TPU v7x, 32 devices: a whole 2x2x4 slice. The times are simulated.
32 devices in a mesh: fsdp: 8 (over y, x, core), tensor: 4 (over z).
Axes of the slice: x: 2, y: 2, z: 4, core: 2. Of those that a mesh axis runs over, the one named last changes fastest.
Arguments:
- out_grad: bfloat16 [256, 8192], P(('fsdp', 'tensor')), may hold values from -6 to 6
- live_rows: int32 [32], P(('fsdp', 'tensor')), may hold values from 1 to 8, as said below
- gate_pre: bfloat16 [256, 12288], P('fsdp', 'tensor'), may hold values from -8 to 8
- up_pre: bfloat16 [256, 12288], P('fsdp', 'tensor'), may hold values from -6 to 6
- down_weight: bfloat16 [12288, 8192], P('tensor', 'fsdp'), may hold values from -0.15625 to 0.15625
- tile_mask: int32 [96, 64], P('tensor'), may hold values from 0 to 1, as said below
Outputs:
- d_gate: bfloat16 [256, 12288], P('fsdp', 'tensor')
- d_up: bfloat16 [256, 12288], P('fsdp', 'tensor')
- d_weight: bfloat16 [12288, 8192], P('tensor', 'fsdp')
Inputs may be any that keep to these rules, and one draw needn't show every extreme that they name: `tile_mask`: each device's shard of 24 x 8 tiles holds 1 to 4 kept tiles; in every draw the shards of some tensor index all hold exactly 4, and every tensor index has a shard holding 4. `live_rows`: some device has all 8 rows live in every draw.
All inputs are finite; a program needn't handle non-finite values.
Results may differ from a plain program's by a relative error of at most 0.015.
Values may be sent and summed in bfloat16 or wider, within the bound.
A program may use at most 64 MiB of HBM per device.

v0:
```python
import math

import jax
import jax.numpy as jnp
from jax import lax
from jax.sharding import PartitionSpec as P

BLK = 128
CAP = 4


def split_count(slot_count):
    group_size = CAP * math.gcd(slot_count // CAP, 8)
    return (group_size, slot_count // group_size)


def per_device(out_grad, live_rows, gate_pre, up_pre, down_weight, tile_mask):
    fsdp_count = lax.axis_size("fsdp")
    fsdp_index = lax.axis_index("fsdp")
    tok_rows = out_grad.shape[0]
    row_blocks = tile_mask.shape[0]
    col_blocks = down_weight.shape[1] // BLK
    local_count = row_blocks * col_blocks
    live_mask = jnp.arange(tok_rows)[:, None] < live_rows[0]
    masked_grad = jnp.where(live_mask, out_grad, jnp.zeros_like(out_grad))
    grad_panel = lax.all_gather(masked_grad, "tensor", axis=0, tiled=True)
    rows_all = grad_panel.shape[0]
    panel_tiles = grad_panel.reshape(rows_all, fsdp_count * col_blocks, BLK)
    shard_masks = (
        tile_mask.reshape(row_blocks, fsdp_count, col_blocks)
        .transpose(1, 0, 2)
        .reshape(fsdp_count, local_count)
    )
    position = jnp.cumsum(shard_masks, axis=1) - 1
    chosen = (shard_masks[:, None, :] == 1) & (
        position[:, None, :] == jnp.arange(CAP)[None, :, None]
    )
    chosen_int = chosen.astype(jnp.int32)
    block_id = jnp.sum(chosen_int * jnp.arange(local_count)[None, None, :], axis=2)
    occupied = jnp.sum(chosen_int, axis=2)
    tile_row = (block_id // col_blocks).reshape(-1)
    tile_col = (jnp.arange(fsdp_count)[:, None] * col_blocks + block_id % col_blocks).reshape(-1)
    tile_live = occupied.reshape(-1).astype(jnp.float32)
    own_choice = lax.dynamic_index_in_dim(chosen_int, fsdp_index, 0, keepdims=False)
    local_tiles = (
        down_weight.reshape(row_blocks, BLK, col_blocks, BLK)
        .transpose(0, 2, 1, 3)
        .reshape(local_count, BLK, BLK)
    )
    packed = jnp.einsum(
        "sb,bij->sij",
        own_choice.astype(jnp.bfloat16),
        local_tiles,
        preferred_element_type=jnp.float32,
    ).astype(jnp.bfloat16)
    gate_value = gate_pre.astype(jnp.float32)
    up_value = up_pre.astype(jnp.float32)
    sigmoid_gate = jax.nn.sigmoid(gate_value)
    hidden = (gate_value * sigmoid_gate * up_value).astype(jnp.bfloat16)
    hidden_tiles = hidden.reshape(rows_all, row_blocks, BLK)
    grad_scale = 1.0 / math.sqrt(rows_all * fsdp_count)
    row_ids = jnp.arange(row_blocks)
    start_sum = jnp.zeros((rows_all, row_blocks, BLK), jnp.float32)
    running_sum = start_sum
    shard_piece = lax.all_gather(packed, "fsdp", axis=0, tiled=True)
    slot_count = shard_piece.shape[0]
    group_size, group_count = split_count(slot_count)
    rows_part = tile_row.reshape(group_count, group_size)
    cols_part = tile_col.reshape(group_count, group_size)

    def add_one_turn(running, parts):
        tile_block, rows_sel, cols_sel = parts
        inputs = jnp.take(panel_tiles, cols_sel, axis=1)
        product = jnp.einsum("rsj,sij->rsi", inputs, tile_block, preferred_element_type=jnp.float32)
        placement = (rows_sel[:, None] == row_ids[None, :]).astype(jnp.float32)
        return (
            running
            + jnp.einsum("rsi,sb->rbi", product, placement, precision=lax.Precision.HIGHEST),
            None,
        )

    running_sum, _ = lax.scan(
        add_one_turn,
        running_sum,
        (shard_piece.reshape(group_count, group_size, BLK, BLK), rows_part, cols_part),
    )
    d_hidden = running_sum.reshape(rows_all, row_blocks * BLK)
    d_up = (d_hidden * gate_value * sigmoid_gate).astype(jnp.bfloat16)
    d_gate = (
        d_hidden * up_value * sigmoid_gate * (1.0 + gate_value * (1.0 - sigmoid_gate))
    ).astype(jnp.bfloat16)
    slot_count = fsdp_count * CAP
    group_size, group_count = split_count(slot_count)
    rows_part = tile_row.reshape(group_count, group_size)
    cols_part = tile_col.reshape(group_count, group_size)
    live_part = tile_live.reshape(group_count, group_size)

    def slot_one_turn(parts):
        rows_sel, cols_sel, live_sel = parts
        left_tiles = jnp.take(hidden_tiles, rows_sel, axis=1)
        right_tiles = jnp.take(panel_tiles, cols_sel, axis=1)
        slot_term = jnp.einsum(
            "rsi,rsj->sij", left_tiles, right_tiles, preferred_element_type=jnp.float32
        )
        return slot_term * (grad_scale * live_sel)[:, None, None]

    own_sums = lax.psum_scatter(
        lax.map(slot_one_turn, (rows_part, cols_part, live_part))
        .reshape(slot_count, BLK, BLK)
        .astype(jnp.bfloat16),
        "fsdp",
        scatter_dimension=0,
        tiled=True,
    ).astype(jnp.float32)
    dense_tiles = jnp.einsum(
        "sb,sij->bij", own_choice.astype(jnp.float32), own_sums, precision=lax.Precision.HIGHEST
    )
    d_weight = dense_tiles.reshape(row_blocks, col_blocks, BLK, BLK).transpose(0, 2, 1, 3)
    d_weight = d_weight.reshape(row_blocks * BLK, col_blocks * BLK).astype(jnp.bfloat16)
    return (d_gate, d_up, d_weight)


def solution(mesh):
    return jax.shard_map(
        per_device,
        mesh=mesh,
        in_specs=(
            P(("fsdp", "tensor"), None),
            P(("fsdp", "tensor")),
            P("fsdp", "tensor"),
            P("fsdp", "tensor"),
            P("tensor", "fsdp"),
            P("tensor", None),
        ),
        out_specs=(P("fsdp", "tensor"), P("fsdp", "tensor"), P("tensor", "fsdp")),
        check_vma=False,
    )
```

profile of v0, /device:TPU:0, one launch (start us, length us, event | category | flops | bytes accessed | tf_op | source)
XLA Modules:
  0.0 112.1 jit_solution(5182315019631317536)
XLA Ops:
  7.2 0.0 all-gather.2.cloned.1.call-start
  7.2 0.8 copy.22
  8.0 0.1 copy.23
  8.1 0.1 broadcast_in_dim_reshape.3
  8.2 0.6 reduce-window.6
  8.8 0.2 slice_reduce_fusion
  9.1 0.1 add_bitcast_fusion
  9.1 4.4 %copy.37 = bf16[384,8,8,128]{3,2,1,0:T(8,128)(2,1)S(1)} copy(bf16[384,8,8,128]{3,1,2,0:T(8,128)(2,1)} %bitcast.71) | data formatting | bytes 12582912
  13.6 0.6 bitcast_bitcast_fusion
  14.2 4.6 %copy.24 = bf16[24,8,128,128]{3,2,1,0:T(8,128)(2,1)} copy(bf16[24,8,128,128]{3,1,2,0:T(8,128)(2,1)S(1)} %bitcast_bitcast_fusion) | data formatting | bytes 12582912 | tf_op jit(solution)/shard_map/transpose | solution.py:47
  18.8 0.0 copy-start.2
  18.8 0.0 copy-start
  18.8 0.0 copy-start.1
  18.8 6.2 %fusion.2 = bf16[4,128,128]{2,0,1:T(4,128)(2,1)S(1)} fusion(bf16[192,128,128]{2,1,0:T(8,128)(2,1)} %bitcast.68, s32[8,4,192]{2,1,0:T(4,128)S(1)} %fusion.28, s32[]{:T(128)S(6)} %select_n.65), kind=kOutput, calls=%fused_computation.9 | convolution fusion | flops 25232128 | bytes 6426628 | tf_op jit(solution)/shard_map/sb,bij->sij/dot_general | solution.py:50
  25.1 0.7 copy.26
  25.8 0.0 all-gather.2.cloned.1.call-update
  25.8 0.0 reduce-scatter.2.cloned.1.call-start
  25.8 0.4 fusion.39
  26.2 0.1 reduce_sum.24
  26.3 0.1 reduce_sum.23
  27.0 0.1 add.83
  27.1 0.1 add.84
  27.2 0.1 mul.75
  27.3 0.0 copy-done.2
  27.3 0.1 broadcast_select_fusion.1
  27.4 17.5 %all_gather.7 = bf16[32,8192]{1,0:T(8,128)(2,1)S(1)} all-gather(bf16[8,8192]{1,0:T(8,128)(2,1)S(1)} %broadcast_select_fusion.1), channel_id=1, replica_groups=mesh['fsdp'=8,'tensor'=4] {'tensor'}, dimensions={0}, use_global_device_ids=true | all-gather | bytes 655360 | tf_op jit(solution)/shard_map/all_gather | solution.py:26
  44.9 0.1 copy_bitcast_fusion.1
  45.0 0.6 gather_fusion.1
  45.7 6.5 %all-gather.2.cloned.1.call-done = bf16[32,128,128]{2,1,0:T(8,128)(2,1)} async-done(((bf16[4,128,128]{2,1,0:T(8,128)(2,1)}), bf16[32,128,128]{2,1,0:T(8,128)(2,1)}) %all-gather.2.cloned.1.call-update) | async-done | bytes 1048592 | tf_op jit(solution)/shard_map/all_gather | solution.py:65
  52.1 1.9 %convolution_bitcast_fusion = f32[32,32,128]{2,0,1:T(8,128)S(1)} fusion(bf16[32,128,128]{2,1,0:T(8,128)(2,1)} %all-gather.2.cloned.1.call-done, bf16[32,32,128]{2,1,0:T(8,128)(2,1)S(1)} %gather_fusion.1, pred[32]{0:T(512)(128)(4,1)S(1)} %get-tuple-element.48), kind=kOutput, calls=%fused_computation.8 | convolution fusion | flops 33685504 | bytes 1835040 | tf_op jit(solution)/shard_map/while/body/eval_jaxpr/rsj,sij->rsi/dot_general | solution.py:74
  54.0 0.7 fusion.5
  54.7 0.0 copy-done
  54.7 0.0 copy-done.1
  54.7 1.0 fusion.16
  55.8 0.6 gather_fusion
  56.4 1.6 %multiply_convert_fusion = bf16[32,128,128]{2,1,0:T(8,128)(2,1)} fusion(f32[32]{0:T(128)S(1)} %mul.75, bf16[32,32,128]{2,1,0:T(8,128)(2,1)S(1)} %gather_fusion, pred[32]{0:T(512)(128)(4,1)S(1)} %get-tuple-element.34, bf16[32,32,128]{2,1,0:T(8,128)(2,1)S(1)} %gather_fusion.1, pred[32]{0:T(512)(128)(4,1)S(1)} %get-tuple-element.48), kind=kOutput, calls=%fused_computation.7 | convolution fusion | flops 34865152 | bytes 1573056 | tf_op jit(solution)/shard_map/while/body/eval_jaxpr/rsi,rsj->sij/dot_general | solution.py:102
  58.0 0.0 reduce-scatter.2.cloned.1.call-update
  58.0 0.1 dot_general.26
  58.1 36.1 %reduce-scatter.2.cloned.1.call-done = bf16[4,128,128]{2,1,0:T(8,128)(2,1)} async-done(((bf16[32,128,128]{2,1,0:T(8,128)(2,1)}), bf16[4,128,128]{2,1,0:T(8,128)(2,1)}) %reduce-scatter.2.cloned.1.call-update) | async-done | bytes 131088 | tf_op jit(solution)/shard_map/reduce_scatter | solution.py:107
  94.2 6.7 %convolution_convert_fusion = bf16[24,8,128,128]{3,1,2,0:T(8,128)(2,1)S(1)} fusion(bf16[4,128,128]{2,1,0:T(8,128)(2,1)} %reduce-scatter.2.cloned.1.call-done, f32[24,8,4,1]{1,0,2,3:T(8,128)S(1)} %bitcast.75), kind=kOutput, calls=%fused_computation.6 | convolution fusion | flops 154140672 | bytes 6425600 | tf_op jit(solution)/shard_map/sb,sij->bij/dot_general | solution.py:115
  100.9 4.3 %copy.57 = bf16[384,8,8,128]{3,1,2,0:T(8,128)(2,1)} copy(bf16[384,8,8,128]{3,2,1,0:T(8,128)(2,1)S(1)} %bitcast.69) | data formatting | bytes 12582912
  (15 shorter events, 0.2 us)
Async XLA Ops:
  7.2 45.0 %all-gather.2.cloned.1.call-start = ((), (), s32[]{:S(2)}) async-start(), calls=%async_computation.1 | async-start | bytes 1179648 | tf_op jit(solution)/shard_map/all_gather | solution.py:65
  18.8 8.5 %copy-start.2 = (bf16[8,8192]{1,0:T(8,128)(2,1)S(1)}, bf16[8,8192]{1,0:T(8,128)(2,1)}, u32[]{:S(2)}) copy-start(bf16[8,8192]{1,0:T(8,128)(2,1)} %param.8) | copy-start | bytes 393220
  18.8 35.9 %copy-start = (bf16[32,3072]{1,0:T(8,128)(2,1)S(1)}, bf16[32,3072]{1,0:T(8,128)(2,1)}, u32[]{:S(2)}) copy-start(bf16[32,3072]{1,0:T(8,128)(2,1)} %param.10) | copy-start | bytes 589828
  18.8 35.9 %copy-start.1 = (bf16[32,3072]{1,0:T(8,128)(2,1)S(1)}, bf16[32,3072]{1,0:T(8,128)(2,1)}, u32[]{:S(2)}) copy-start(bf16[32,3072]{1,0:T(8,128)(2,1)} %param.11) | copy-start | bytes 589828
  25.8 68.4 %reduce-scatter.2.cloned.1.call-start = ((), (), s32[]{:S(2)}) async-start(), calls=%async_computation.2 | async-start | bytes 1179648 | tf_op jit(solution)/shard_map/reduce_scatter | solution.py:107
Sparse Core Ops, SparseCore 0:
  25.9 26.1 all-gather.1
  58.1 36.0 reduce-scatter.1
where the time goes:
time: 112 us
  waiting for transfers between devices  42.6 us (38%)
  local copies, waits for them, and re-layouts  17.7 us (16%)
  blocking collectives  17.5 us (16%)
  matrix products  17.1 us (15%)
  between operations  14.9 us (13%)
  other arithmetic  2.21 us (2%)
    reduce_scatter x1, waiting for transfers between devices, per_device(): lax.psum_scatter(lax.map(slot_one_turn, (rows_part, cols_part, live_part)...  36.1 us
    all_gather x1, blocking collectives, per_device(): grad_panel = lax.all_gather(masked_grad, 'tensor', axis=0, tiled=True)  17.5 us
    unnamed x9, local copies, waits for them, and re-layouts  9.55 us
    dot_general x1, matrix products, per_device(): jnp.einsum('sb,sij->bij', own_choice.astype(jnp.float32), own_sums, preci...  6.69 us
    all_gather x1, waiting for transfers between devices, per_device(): shard_piece = lax.all_gather(packed, 'fsdp', axis=0, tiled=True)  6.46 us
    dot_general x1, matrix products, per_device(): jnp.einsum('sb,bij->sij', own_choice.astype(jnp.bfloat16), local_tiles, p...  6.25 us
    transpose x2, local copies, waits for them, and re-layouts, per_device(): local_tiles = down_weight.reshape(row_blocks, BLK, col_blocks, BLK).trans...  5.23 us
  transfers between devices with their start and end apart: 2, of which 2 were waited for; matrix products, arithmetic and copies ran while one was open for 1% of the time, Pallas kernels for 0%

commit v1 on v0

v1 whole, which is shorter than its diff:
```python
import functools
import math

import jax
import jax.numpy as jnp
from jax import lax
from jax.experimental import pallas as pl
from jax.experimental.pallas import tpu as pltpu
from jax.sharding import PartitionSpec as P

BLK = 128
CAP = 4
MESH = pl.DeviceIdType.MESH
F32 = jnp.float32
BF16 = jnp.bfloat16


def tile_lists(mask, row_blocks, cols):
    shift = cols.bit_length() - 1
    row_count, lanes = mask.shape
    empty = row_count * cols
    row_id = lax.broadcasted_iota(jnp.int32, mask.shape, 0)
    lane = lax.broadcasted_iota(jnp.int32, mask.shape, 1)
    code = jnp.where(mask == 1, row_id * cols + (lane & (cols - 1)), empty)
    shard = lax.shift_right_logical(lane, shift)
    out_row = lax.broadcasted_iota(jnp.int32, (16, BLK), 0)
    out_lane = lax.broadcasted_iota(jnp.int32, (16, BLK), 1)
    found = jnp.full((16, BLK), empty, jnp.int32)
    slot = out_row & (CAP - 1)
    for g in range(lanes // cols):
        own = jnp.where(shard == g, code, empty)
        for k in range(CAP):
            least = jnp.min(jnp.min(own, axis=0, keepdims=True), axis=1, keepdims=True)
            found = jnp.where((slot == k) & (out_lane == g), least, found)
            own = jnp.where(own == least, empty, own)
    row = jnp.minimum(lax.shift_right_logical(found, shift), row_blocks - 1)
    live = jnp.where(found < empty, 1, 0)
    return jnp.where(out_row < CAP, row, jnp.where(out_row < 2 * CAP, found & (cols - 1), live))


def exchange_kernel(
    fs, ts, cols, scale,
    live_ref, grad_ref, gate_ref, up_ref, mask_ref, w_hbm,
    pr_out, dw_out, idx_out,
    chunk, chunk_in, panel, z_send, z_in, hid, hid_send, hid_in, prod, prod_in, w_vmem, idx_v, idx_s,
    w_sem, idx_sem, i_send, i_recv, a_send, a_recv, b_send, b_recv, h_send, h_recv, p_send, p_recv,
):
    f = lax.axis_index("fsdp")
    t = lax.axis_index("tensor")
    tok = grad_ref.shape[0]
    row_blocks, rows = hid.shape[0], hid.shape[1]
    compact = cols > CAP
    held = z_in.shape[1]

    def f_peer(j):
        return lax.rem(f + j, fs)

    def t_peer(j):
        return lax.rem(t + j, ts)

    def tile_row(k, g):
        return idx_s[t, k, g]

    def tile_col(u, k):
        return idx_s[u, CAP + k, f]

    barrier = pltpu.get_barrier_semaphore()
    for j in range(1, fs):
        pl.semaphore_signal(barrier, inc=1, device_id={"fsdp": f_peer(j)}, device_id_type=MESH)
    for j in range(1, ts):
        pl.semaphore_signal(barrier, inc=1, device_id={"tensor": t_peer(j)}, device_id_type=MESH)
    w_copies = []
    for c in range(cols):
        copy = pltpu.make_async_copy(w_hbm.at[:, :, c * BLK : (c + 1) * BLK], w_vmem.at[c], w_sem.at[c])
        copy.start()
        w_copies.append(copy)

    live = lax.broadcasted_iota(jnp.int32, (tok, BLK), 0) < live_ref[0]
    for g in range(fs):
        parts = []
        for c in range(cols):
            at = (g * cols + c) * BLK
            parts.append(jnp.where(live, grad_ref[:, at : at + BLK].astype(F32), 0.0))
        chunk[g] = jnp.concatenate(parts, axis=0).astype(BF16)
    lists = tile_lists(mask_ref[...], row_blocks, cols)
    idx_out[...] = lists
    idx_v[t] = lists

    pl.semaphore_wait(barrier, fs - 1 + ts - 1)

    def over_fsdp(src, dst, send, recv):
        copies = []
        for j in range(1, fs):
            copy = pltpu.make_async_remote_copy(
                src_ref=src.at[f_peer(j)],
                dst_ref=dst.at[f],
                send_sem=send.at[j],
                recv_sem=recv.at[j],
                device_id={"fsdp": f_peer(j)},
                device_id_type=MESH,
            )
            copy.start()
            copies.append(copy)
        return copies

    a_copies = over_fsdp(chunk, chunk_in, a_send, a_recv)
    i_copies = []
    for j in range(1, ts):
        copy = pltpu.make_async_remote_copy(
            src_ref=idx_v.at[t],
            dst_ref=idx_v.at[t],
            send_sem=i_send.at[j],
            recv_sem=i_recv.at[j],
            device_id={"tensor": t_peer(j)},
            device_id_type=MESH,
        )
        copy.start()
        i_copies.append(copy)
    chunk_in[f] = chunk[f]

    for r in range(row_blocks):
        gate = gate_ref[:, r * BLK : (r + 1) * BLK].astype(F32)
        up = up_ref[:, r * BLK : (r + 1) * BLK].astype(F32)
        hid[r] = (gate * jax.nn.sigmoid(gate) * up).astype(BF16)

    for copy in i_copies:
        copy.wait_recv()
    idx_copy = pltpu.make_async_copy(idx_v, idx_s, idx_sem)
    idx_copy.start()

    for copy in a_copies:
        copy.wait_recv()
    wide = [chunk_in[g].astype(F32) for g in range(fs)]
    for c in range(cols):
        panel[c] = jnp.concatenate([w[c * tok : (c + 1) * tok] for w in wide], axis=0).astype(BF16)
    idx_copy.wait()

    b_copies = []
    for j in range(1, ts):
        if compact:
            for k in range(CAP):
                z_send[j, k] = panel[tile_col(t_peer(j), k)]
        copy = pltpu.make_async_remote_copy(
            src_ref=z_send.at[j] if compact else panel,
            dst_ref=z_in.at[t],
            send_sem=b_send.at[j],
            recv_sem=b_recv.at[j],
            device_id={"tensor": t_peer(j)},
            device_id_type=MESH,
        )
        copy.start()
        b_copies.append(copy)
    for k in range(held):
        z_in[t, k] = panel[tile_col(t, k)] if compact else panel[k]

    for g in range(fs):
        for k in range(CAP):
            hid_send[g, k] = hid[tile_row(k, g)]
    h_copies = over_fsdp(hid_send, hid_in, h_send, h_recv)
    hid_in[f] = hid_send[f]

    for copy in w_copies:
        copy.wait()
    for copy in b_copies:
        copy.wait_recv()
    grads = []
    for k in range(CAP):
        col = tile_col(t, k)
        slot = k if compact else col
        wide = [z_in[u, slot].astype(F32) for u in range(ts)]
        pieces = [w[g * tok : (g + 1) * tok] for g in range(fs) for w in wide]
        grad = jnp.concatenate(pieces, axis=0).astype(BF16)
        grads.append(grad)
        tile = w_vmem[col, tile_row(k, f)]
        out = lax.dot_general(grad, tile, (((1,), (1,)), ((), ())), preferred_element_type=F32)
        out = out.astype(BF16)
        for g in range(fs):
            prod[g, k] = out[g * rows : (g + 1) * rows]
    p_copies = over_fsdp(prod, prod_in, p_send, p_recv)
    prod_in[f] = prod[f]

    for copy in h_copies:
        copy.wait_recv()
    for k in range(CAP):
        left = jnp.concatenate([hid_in[g, k] for g in range(fs)], axis=0)
        total = lax.dot_general(left, grads[k], (((0,), (0,)), ((), ())), preferred_element_type=F32)
        dw_out[k] = (total * scale).astype(BF16)
    for copy in p_copies:
        copy.wait_recv()
    pr_out[...] = prod_in[...]
    for copy in i_copies + a_copies + b_copies + h_copies + p_copies:
        copy.wait_send()


def finish_kernel(
    fs, idx_ref, prod_ref, dw_ref, gate_ref, up_ref, d_gate, d_up, d_weight, acc, blank, z_sem, t_sem
):
    row_blocks = acc.shape[0]
    blank[...] = jnp.zeros_like(blank)
    fills = []
    for r in range(row_blocks):
        fill = pltpu.make_async_copy(blank, d_weight.at[pl.ds(r * BLK, BLK)], z_sem.at[r])
        fill.start()
        fills.append(fill)
    acc[...] = jnp.zeros_like(acc)
    for g in range(fs):
        for k in range(CAP):
            row = idx_ref[k, g]
            weight = idx_ref[2 * CAP + k, g].astype(F32)
            acc[row] += prod_ref[g, k].astype(F32) * weight
    for r in range(row_blocks):
        at = slice(r * BLK, (r + 1) * BLK)
        gate = gate_ref[:, at].astype(F32)
        up = up_ref[:, at].astype(F32)
        sig = jax.nn.sigmoid(gate)
        d_hidden = acc[r]
        d_up[:, at] = (d_hidden * gate * sig).astype(BF16)
        d_gate[:, at] = (d_hidden * up * sig * (1.0 + gate * (1.0 - sig))).astype(BF16)
    for fill in fills:
        fill.wait()
    f = lax.axis_index("fsdp")

    def place(k):
        row_at = pl.multiple_of(idx_ref[k, f] * BLK, BLK)
        col_at = pl.multiple_of(idx_ref[CAP + k, f] * BLK, BLK)
        return pltpu.make_async_copy(
            dw_ref.at[k], d_weight.at[pl.ds(row_at, BLK), pl.ds(col_at, BLK)], t_sem.at[k]
        )

    for k in range(CAP):
        @pl.when(idx_ref[2 * CAP + k, f] > 0)
        def _():
            place(k).start()

    for k in range(CAP):
        @pl.when(idx_ref[2 * CAP + k, f] > 0)
        def _():
            place(k).wait()


def per_device(out_grad, live_rows, gate_pre, up_pre, down_weight, tile_mask):
    fs = lax.axis_size("fsdp")
    ts = lax.axis_size("tensor")
    tok = out_grad.shape[0]
    rows = gate_pre.shape[0]
    row_blocks = tile_mask.shape[0]
    cols = down_weight.shape[1] // BLK
    held = min(cols, CAP)
    scale = 1.0 / math.sqrt(rows * fs)
    mask = tile_mask
    if row_blocks % 8:
        mask = jnp.pad(tile_mask, ((0, 8 - row_blocks % 8), (0, 0)))
    vmem = pl.BlockSpec(memory_space=pltpu.VMEM)
    smem = pl.BlockSpec(memory_space=pltpu.SMEM)
    hbm = pl.BlockSpec(memory_space=pltpu.HBM)
    slots = (fs, CAP, rows, BLK)
    dma = pltpu.SemaphoreType.DMA
    prod, tiles, lists = pl.pallas_call(
        functools.partial(exchange_kernel, fs, ts, cols, scale),
        out_shape=(
            jax.ShapeDtypeStruct(slots, BF16),
            jax.ShapeDtypeStruct((CAP, BLK, BLK), BF16),
            jax.ShapeDtypeStruct((16, BLK), jnp.int32),
        ),
        in_specs=[smem, vmem, vmem, vmem, vmem, hbm],
        out_specs=(vmem, vmem, vmem),
        scratch_shapes=[
            pltpu.VMEM((fs, cols * tok, BLK), BF16),
            pltpu.VMEM((fs, cols * tok, BLK), BF16),
            pltpu.VMEM((cols, fs * tok, BLK), BF16),
            pltpu.VMEM((ts, held, fs * tok, BLK), BF16),
            pltpu.VMEM((ts, held, fs * tok, BLK), BF16),
            pltpu.VMEM((row_blocks, rows, BLK), BF16),
            pltpu.VMEM(slots, BF16),
            pltpu.VMEM(slots, BF16),
            pltpu.VMEM(slots, BF16),
            pltpu.VMEM(slots, BF16),
            pltpu.VMEM((cols, row_blocks, BLK, BLK), BF16),
            pltpu.VMEM((ts, 16, BLK), jnp.int32),
            pltpu.SMEM((ts, 16, BLK), jnp.int32),
            dma((cols,)),
            dma,
            dma((ts,)),
            dma((ts,)),
            dma((fs,)),
            dma((fs,)),
            dma((ts,)),
            dma((ts,)),
            dma((fs,)),
            dma((fs,)),
            dma((fs,)),
            dma((fs,)),
        ],
        compiler_params=pltpu.CompilerParams(
            collective_id=0, has_side_effects=True, vmem_limit_bytes=48 * 1024 * 1024
        ),
        name="exchange",
    )(live_rows, out_grad, gate_pre, up_pre, mask, down_weight.reshape(row_blocks, BLK, cols * BLK))
    return pl.pallas_call(
        functools.partial(finish_kernel, fs),
        out_shape=(
            jax.ShapeDtypeStruct(gate_pre.shape, BF16),
            jax.ShapeDtypeStruct(up_pre.shape, BF16),
            jax.ShapeDtypeStruct(down_weight.shape, BF16),
        ),
        in_specs=[smem, vmem, vmem, vmem, vmem],
        out_specs=(vmem, vmem, hbm),
        scratch_shapes=[
            pltpu.VMEM((row_blocks, rows, BLK), F32),
            pltpu.VMEM((BLK, down_weight.shape[1]), BF16),
            dma((row_blocks,)),
            dma((CAP,)),
        ],
        compiler_params=pltpu.CompilerParams(vmem_limit_bytes=32 * 1024 * 1024),
        name="finish",
    )(lists, prod, tiles, gate_pre, up_pre)


def solution(mesh):
    return jax.shard_map(
        per_device,
        mesh=mesh,
        in_specs=(
            P(("fsdp", "tensor"), None),
            P(("fsdp", "tensor")),
            P("fsdp", "tensor"),
            P("fsdp", "tensor"),
            P("tensor", "fsdp"),
            P("tensor", None),
        ),
        out_specs=(P("fsdp", "tensor"), P("fsdp", "tensor"), P("tensor", "fsdp")),
        check_vma=False,
    )
```

time: 112 us -> 30.7 us (0.27)
  waiting for transfers between devices: 42.6 us -> 0 us
  Pallas kernels: 0 us -> 25.7 us
  blocking collectives: 17.5 us -> 0 us
  matrix products: 17.1 us -> 0 us
  local copies, waits for them, and re-layouts: 17.7 us -> 3.46 us
  between operations: 14.9 us -> 1.3 us
  other arithmetic: 2.21 us -> 0 us
    reduce_scatter x1 -> x0, waiting for transfers between devices: 36.1 us -> none  [per_device(): lax.psum_scatter(lax.map(slot_one_turn, (rows_part, cols_part, live_part)...]
    pallas_call x0 -> x2, Pallas kernels: none -> 25.7 us  [the longest x1 20.8 us: per_device(): pl.pallas_call(functools.partial(exchange_kernel, fs, ts, cols, scale), o...]
    all_gather x1 -> x0, blocking collectives: 17.5 us -> none  [per_device(): grad_panel = lax.all_gather(masked_grad, 'tensor', axis=0, tiled=True)]
    dot_general x5 -> x0, matrix products: 17.1 us -> none  [the longest x1 6.69 us: per_device(): jnp.einsum('sb,sij->bij', own_choice.astype(jnp.float32), own_sums, preci...]
    all_gather x1 -> x0, waiting for transfers between devices: 6.46 us -> none  [per_device(): shard_piece = lax.all_gather(packed, 'fsdp', axis=0, tiled=True)]
    unnamed x9 -> x8, local copies, waits for them, and re-layouts: 9.55 us -> 3.46 us
    transpose x3 -> x0, local copies, waits for them, and re-layouts: 5.32 us -> none  [the longest x2 5.23 us: per_device(): local_tiles = down_weight.reshape(row_blocks, BLK, col_blocks, BLK).trans...]
    gather x2 -> x0, local copies, waits for them, and re-layouts: 1.2 us -> none  [the longest x1 0.6 us: add_one_turn(): inputs = jnp.take(panel_tiles, cols_sel, axis=1)]
  transfers between devices with their start and end apart: 2 -> 0, of which waited for: 2 -> 0; matrix products, arithmetic and copies ran while one was open for 1% -> 0% of each run, Pallas kernels for 0% -> 0%
where the time goes in v1:
time: 30.7 us; the launch traced here: 30.5 us
  Pallas kernels  25.7 us (84%)
  local copies, waits for them, and re-layouts  3.46 us (11%)
  between operations  1.3 us (4%)
    pallas_call x1, Pallas kernels, per_device(): pl.pallas_call(functools.partial(exchange_kernel, fs, ts, cols, scale), o...  20.8 us
    pallas_call x1, Pallas kernels, per_device(): pl.pallas_call(functools.partial(finish_kernel, fs), out_shape=(jax.Shape...  4.95 us
    unnamed x8, local copies, waits for them, and re-layouts  3.46 us

profile of v1, /device:TPU:0, one launch (start us, length us, event | category | flops | bytes accessed | tf_op | source)
XLA Modules:
  0.0 30.5 jit_solution(14855121177936460539)
XLA Ops:
  1.3 0.0 copy-start
  1.3 0.9 %copy-done = bf16[32,3072]{1,0:T(8,128)(2,1)S(1)} copy-done((bf16[32,3072]{1,0:T(8,128)(2,1)S(1)}, bf16[32,3072]{1,0:T(8,128)(2,1)}, u32[]{:S(2)}) %copy-start) | copy-done | bytes 196632
  2.2 0.0 copy-start.1
  2.2 0.9 %copy-done.1 = bf16[32,3072]{1,0:T(8,128)(2,1)S(1)} copy-done((bf16[32,3072]{1,0:T(8,128)(2,1)S(1)}, bf16[32,3072]{1,0:T(8,128)(2,1)}, u32[]{:S(2)}) %copy-start.1) | copy-done | bytes 196632
  3.1 0.0 copy-start.2
  3.1 0.9 %copy-done.2 = bf16[8,8192]{1,0:T(8,128)(2,1)S(1)} copy-done((bf16[8,8192]{1,0:T(8,128)(2,1)S(1)}, bf16[8,8192]{1,0:T(8,128)(2,1)}, u32[]{:S(2)}) %copy-start.2) | copy-done | bytes 131096
  4.0 0.0 copy-start.3
  4.0 0.7 %copy-done.3 = s32[24,64]{1,0:T(8,128)S(1)} copy-done((s32[24,64]{1,0:T(8,128)S(1)}, s32[24,64]{1,0:T(8,128)}, u32[]{:S(2)}) %copy-start.3) | copy-done | bytes 6168
  4.7 20.8 %exchange.1 = (bf16[8,4,32,128]{3,2,1,0:T(8,128)(2,1)S(1)}, bf16[4,128,128]{2,1,0:T(8,128)(2,1)S(1)}, s32[16,128]{1,0:T(8,128)S(1)}) custom-call(s32[1]{0:T(128)S(6)} %copy.9.live_ref, bf16[8,8192]{1,0:T(8,128)(2,1)S(1)} %copy-done.2, bf16[32,3072]{1,0:T(8,128)(2,1)S(1)} %copy-done, bf16[32,3072]{1,0:T(8,128)(2,1)S(1)} %copy-done.1, s32[24,64]{1,0:T(8,128)S(1)} %copy-done.3, ...), custom_call_target="tpu_custom_call" | custom-call | tf_op jit(solution)/shard_map/exchange/pallas_call | solution.py:258
  25.5 4.9 %finish.1 = (bf16[32,3072]{1,0:T(8,128)(2,1)}, bf16[32,3072]{1,0:T(8,128)(2,1)}, bf16[3072,1024]{1,0:T(8,128)(2,1)}) custom-call(s32[16,128]{1,0:T(8,128)S(1)} %get-tuple-element.6.idx_ref, bf16[8,4,32,128]{3,2,1,0:T(8,128)(2,1)S(1)} %get-tuple-element.7.prod_ref, bf16[4,128,128]{2,1,0:T(8,128)(2,1)S(1)} %get-tuple-element.8.dw_ref, ...), custom_call_target="tpu_custom_call" | custom-call | tf_op jit(solution)/shard_map/finish/pallas_call | solution.py:299
Async XLA Ops:
  1.3 0.9 %copy-start = (bf16[32,3072]{1,0:T(8,128)(2,1)S(1)}, bf16[32,3072]{1,0:T(8,128)(2,1)}, u32[]{:S(2)}) copy-start(bf16[32,3072]{1,0:T(8,128)(2,1)} %gate_ref.3) | copy-start | bytes 589828
  2.2 0.9 %copy-start.1 = (bf16[32,3072]{1,0:T(8,128)(2,1)S(1)}, bf16[32,3072]{1,0:T(8,128)(2,1)}, u32[]{:S(2)}) copy-start(bf16[32,3072]{1,0:T(8,128)(2,1)} %up_ref.3) | copy-start | bytes 589828
  3.1 0.9 %copy-start.2 = (bf16[8,8192]{1,0:T(8,128)(2,1)S(1)}, bf16[8,8192]{1,0:T(8,128)(2,1)}, u32[]{:S(2)}) copy-start(bf16[8,8192]{1,0:T(8,128)(2,1)} %grad_ref.1) | copy-start | bytes 393220
  4.0 0.7 %copy-start.3 = (s32[24,64]{1,0:T(8,128)S(1)}, s32[24,64]{1,0:T(8,128)}, u32[]{:S(2)}) copy-start(s32[24,64]{1,0:T(8,128)} %mask_ref.1) | copy-start | bytes 18436

commit v2 on v1

v2 whole, which is shorter than its diff:
```python
import functools
import math

import jax
import jax.numpy as jnp
from jax import lax
from jax.experimental import pallas as pl
from jax.experimental.pallas import tpu as pltpu
from jax.sharding import PartitionSpec as P

BLK = 128
CAP = 4
MESH = pl.DeviceIdType.MESH
F32 = jnp.float32
BF16 = jnp.bfloat16


def tile_lists(mask, row_blocks, cols):
    shift = cols.bit_length() - 1
    row_count, lanes = mask.shape
    empty = row_count * cols
    row_id = lax.broadcasted_iota(jnp.int32, mask.shape, 0)
    lane = lax.broadcasted_iota(jnp.int32, mask.shape, 1)
    code = jnp.where(mask == 1, row_id * cols + (lane & (cols - 1)), empty)
    shard = lax.shift_right_logical(lane, shift)
    out_row = lax.broadcasted_iota(jnp.int32, (16, BLK), 0)
    out_lane = lax.broadcasted_iota(jnp.int32, (16, BLK), 1)
    found = jnp.full((16, BLK), empty, jnp.int32)
    slot = out_row & (CAP - 1)
    for g in range(lanes // cols):
        own = jnp.where(shard == g, code, empty)
        for k in range(CAP):
            least = jnp.min(jnp.min(own, axis=0, keepdims=True), axis=1, keepdims=True)
            found = jnp.where((slot == k) & (out_lane == g), least, found)
            own = jnp.where(own == least, empty, own)
    row = jnp.minimum(lax.shift_right_logical(found, shift), row_blocks - 1)
    live = jnp.where(found < empty, 1, 0)
    return jnp.where(out_row < CAP, row, jnp.where(out_row < 2 * CAP, found & (cols - 1), live))


def exchange_kernel(
    fs, ts, cols, scale,
    live_ref, grad_hbm, gate_hbm, up_hbm, mask_hbm, w_hbm,
    pr_out, dw_out, idx_out,
    grad_ref, gate_ref, up_ref, mask_ref, dw,
    chunk, chunk_in, panel, z_send, z_in, hid, hid_send, hid_in, prod, prod_in, w_vmem, idx_v, idx_s,
    in_sem, out_sem, w_sem, idx_sem, i_send, i_recv, a_send, a_recv, b_send, b_recv, h_send, h_recv, p_send, p_recv,
):
    f = lax.axis_index("fsdp")
    t = lax.axis_index("tensor")
    tok = grad_ref.shape[0]
    row_blocks, rows = hid.shape[0], hid.shape[1]
    compact = cols > CAP
    groups, per_z = z_in.shape[0], z_in.shape[2]
    per_p = prod.shape[2]

    def f_peer(j):
        return lax.rem(f + j, fs)

    def t_peer(j):
        return lax.rem(t + j, ts)

    def tile_row(k, g):
        return idx_s[t, k, g]

    def tile_col(u, k):
        return idx_s[u, CAP + k, f]

    loads = [
        pltpu.make_async_copy(src, dst, in_sem.at[n])
        for n, (src, dst) in enumerate(
            ((grad_hbm, grad_ref), (mask_hbm, mask_ref), (gate_hbm, gate_ref), (up_hbm, up_ref))
        )
    ]
    for copy in loads:
        copy.start()
    barrier = pltpu.get_barrier_semaphore()
    for j in range(1, fs):
        pl.semaphore_signal(barrier, inc=1, device_id={"fsdp": f_peer(j)}, device_id_type=MESH)
    for j in range(1, ts):
        pl.semaphore_signal(barrier, inc=1, device_id={"tensor": t_peer(j)}, device_id_type=MESH)

    live = lax.broadcasted_iota(jnp.int32, (tok, BLK), 0) < live_ref[0]
    loads[0].wait()
    for g in range(fs):
        parts = []
        for c in range(cols):
            at = (g * cols + c) * BLK
            parts.append(jnp.where(live, grad_ref[:, at : at + BLK].astype(F32), 0.0))
        chunk[g] = jnp.concatenate(parts, axis=0).astype(BF16)

    pl.semaphore_wait(barrier, fs - 1 + ts - 1)

    def remote(src, dst, send, recv, peer):
        copy = pltpu.make_async_remote_copy(
            src_ref=src, dst_ref=dst, send_sem=send, recv_sem=recv, device_id=peer, device_id_type=MESH
        )
        copy.start()
        return copy

    def over_fsdp(src, dst, send, recv):
        return [
            remote(src.at[f_peer(j)], dst.at[f], send.at[j], recv.at[j], {"fsdp": f_peer(j)})
            for j in range(1, fs)
        ]

    a_copies = over_fsdp(chunk, chunk_in, a_send, a_recv)
    loads[1].wait()
    lists = tile_lists(mask_ref[...], row_blocks, cols)
    idx_v[t] = lists
    outs = [pltpu.make_async_copy(idx_v.at[t], idx_out, out_sem.at[0])]
    outs[0].start()
    i_copies = [
        remote(idx_v.at[t], idx_v.at[t], i_send.at[j], i_recv.at[j], {"tensor": t_peer(j)})
        for j in range(1, ts)
    ]
    w_copies = []
    for c in range(cols):
        copy = pltpu.make_async_copy(w_hbm.at[:, :, c * BLK : (c + 1) * BLK], w_vmem.at[c], w_sem.at[c])
        copy.start()
        w_copies.append(copy)
    chunk_in[f] = chunk[f]

    for copy in loads[2:]:
        copy.wait()
    for r in range(row_blocks):
        gate = gate_ref[:, r * BLK : (r + 1) * BLK].astype(F32)
        up = up_ref[:, r * BLK : (r + 1) * BLK].astype(F32)
        hid[r] = (gate * jax.nn.sigmoid(gate) * up).astype(BF16)

    for copy in i_copies:
        copy.wait_recv()
    idx_copy = pltpu.make_async_copy(idx_v, idx_s, idx_sem)
    idx_copy.start()

    for copy in a_copies:
        copy.wait_recv()
    wide = [chunk_in[g].astype(F32) for g in range(fs)]
    for c in range(cols):
        panel[c] = jnp.concatenate([w[c * tok : (c + 1) * tok] for w in wide], axis=0).astype(BF16)
    idx_copy.wait()

    b_copies = []
    for q in range(groups):
        sent = []
        for j in range(1, ts):
            for k in range(per_z):
                if compact:
                    z_send[q, j, k] = panel[tile_col(t_peer(j), q * per_z + k)]
            sent.append(
                remote(
                    z_send.at[q, j] if compact else panel,
                    z_in.at[q, t],
                    b_send.at[q, j],
                    b_recv.at[q, j],
                    {"tensor": t_peer(j)},
                )
            )
        b_copies.append(sent)

    for g in range(fs):
        for k in range(CAP):
            hid_send[g, k] = hid[tile_row(k, g)]
    h_copies = over_fsdp(hid_send, hid_in, h_send, h_recv)
    hid_in[f] = hid_send[f]
    for q in range(groups):
        for k in range(per_z):
            z_in[q, t, k] = panel[tile_col(t, q * per_z + k)] if compact else panel[k]

    for copy in w_copies:
        copy.wait()
    grads = []
    p_copies = []
    for q in range(groups):
        for copy in b_copies[q]:
            copy.wait_recv()
        for m in range(per_p):
            k = q * per_p + m
            slot = m if compact else tile_col(t, k)
            wide = [z_in[q, u, slot].astype(F32) for u in range(ts)]
            pieces = [w[g * tok : (g + 1) * tok] for g in range(fs) for w in wide]
            grad = jnp.concatenate(pieces, axis=0).astype(BF16)
            grads.append(grad)
            tile = w_vmem[tile_col(t, k), tile_row(k, f)]
            out = lax.dot_general(grad, tile, (((1,), (1,)), ((), ())), preferred_element_type=F32)
            out = out.astype(BF16)
            for g in range(fs):
                prod[q, g, m] = out[g * rows : (g + 1) * rows]
        p_copies += over_fsdp(prod.at[q], prod_in.at[q], p_send.at[q], p_recv.at[q])
        prod_in[q, f] = prod[q, f]

    for copy in h_copies:
        copy.wait_recv()
    for k in range(CAP):
        left = jnp.concatenate([hid_in[g, k] for g in range(fs)], axis=0)
        total = lax.dot_general(left, grads[k], (((0,), (0,)), ((), ())), preferred_element_type=F32)
        dw[k] = (total * scale).astype(BF16)
    outs.append(pltpu.make_async_copy(dw, dw_out, out_sem.at[1]))
    outs[1].start()
    sent = [copy for group in b_copies for copy in group]
    for copy in i_copies + a_copies + sent + h_copies:
        copy.wait_send()
    for copy in p_copies:
        copy.wait_recv()
    outs.append(pltpu.make_async_copy(prod_in, pr_out, out_sem.at[2]))
    outs[2].start()
    for copy in p_copies:
        copy.wait_send()
    for copy in outs:
        copy.wait()


def finish_kernel(
    fs, idx_ref, prod_hbm, dw_hbm, gate_hbm, up_hbm, d_gate_hbm, d_up_hbm, d_weight,
    prod_ref, dw_ref, gate_ref, up_ref, acc, blank, tiled, d_gate, d_up, in_sem, z_sem, t_sem, o_sem,
):
    loads = [
        pltpu.make_async_copy(src, dst, in_sem.at[n])
        for n, (src, dst) in enumerate(
            ((dw_hbm, dw_ref), (prod_hbm, prod_ref), (gate_hbm, gate_ref), (up_hbm, up_ref))
        )
    ]
    for copy in loads:
        copy.start()
    row_blocks = acc.shape[0]
    f = lax.axis_index("fsdp")
    row_of = [idx_ref[k, f] for k in range(CAP)]
    col_of = [idx_ref[CAP + k, f] for k in range(CAP)]
    live = [idx_ref[2 * CAP + k, f] > 0 for k in range(CAP)]
    first = []
    for k in range(CAP):
        fresh = live[k]
        for m in range(k):
            fresh = fresh & jnp.logical_not(live[m] & (row_of[m] == row_of[k]))
        first.append(fresh)

    def bare(r):
        clear = None
        for k in range(CAP):
            off = jnp.logical_not(live[k] & (row_of[k] == r))
            clear = off if clear is None else clear & off
        return clear

    def fill(r):
        return pltpu.make_async_copy(blank, d_weight.at[pl.ds(r * BLK, BLK)], z_sem.at[r])

    def place(k):
        row_at = pl.multiple_of(row_of[k] * BLK, BLK)
        return pltpu.make_async_copy(tiled.at[k], d_weight.at[pl.ds(row_at, BLK)], t_sem.at[k])

    blank[...] = jnp.zeros_like(blank)
    for r in range(row_blocks):
        @pl.when(bare(r))
        def _():
            fill(r).start()

    tiled[...] = jnp.zeros_like(tiled)
    loads[0].wait()
    for k in range(CAP):
        for m in range(CAP):
            @pl.when(live[m] & (row_of[m] == row_of[k]))
            def _():
                tiled[k, :, pl.ds(pl.multiple_of(col_of[m] * BLK, BLK), BLK)] = dw_ref[m]

        @pl.when(first[k])
        def _():
            place(k).start()

    acc[...] = jnp.zeros_like(acc)
    for copy in loads[1:]:
        copy.wait()
    for g in range(fs):
        for k in range(CAP):
            row = idx_ref[k, g]
            weight = idx_ref[2 * CAP + k, g].astype(F32)
            per = prod_ref.shape[2]
            acc[row] += prod_ref[k // per, g, k % per].astype(F32) * weight
    for r in range(row_blocks):
        at = slice(r * BLK, (r + 1) * BLK)
        gate = gate_ref[:, at].astype(F32)
        up = up_ref[:, at].astype(F32)
        sig = jax.nn.sigmoid(gate)
        d_hidden = acc[r]
        d_up[:, at] = (d_hidden * gate * sig).astype(BF16)
        d_gate[:, at] = (d_hidden * up * sig * (1.0 + gate * (1.0 - sig))).astype(BF16)
    outs = [
        pltpu.make_async_copy(d_gate, d_gate_hbm, o_sem.at[0]),
        pltpu.make_async_copy(d_up, d_up_hbm, o_sem.at[1]),
    ]
    for copy in outs:
        copy.start()
    for r in range(row_blocks):
        @pl.when(bare(r))
        def _():
            fill(r).wait()

    for k in range(CAP):
        @pl.when(first[k])
        def _():
            place(k).wait()

    for copy in outs:
        copy.wait()


def per_device(out_grad, live_rows, gate_pre, up_pre, down_weight, tile_mask):
    fs = lax.axis_size("fsdp")
    ts = lax.axis_size("tensor")
    tok = out_grad.shape[0]
    rows = gate_pre.shape[0]
    row_blocks = tile_mask.shape[0]
    cols = down_weight.shape[1] // BLK
    groups = 2 if cols > CAP else 1
    per_z = CAP // groups if cols > CAP else cols
    scale = 1.0 / math.sqrt(rows * fs)
    mask = tile_mask
    if row_blocks % 8:
        mask = jnp.pad(tile_mask, ((0, 8 - row_blocks % 8), (0, 0)))
    smem = pl.BlockSpec(memory_space=pltpu.SMEM)
    hbm = pl.BlockSpec(memory_space=pltpu.HBM)
    slots = (fs, CAP, rows, BLK)
    halves = (groups, fs, CAP // groups, rows, BLK)
    blocks = (row_blocks, rows, BLK)
    dma = pltpu.SemaphoreType.DMA
    prod, tiles, lists = pl.pallas_call(
        functools.partial(exchange_kernel, fs, ts, cols, scale),
        out_shape=(
            jax.ShapeDtypeStruct(halves, BF16),
            jax.ShapeDtypeStruct((CAP, BLK, BLK), BF16),
            jax.ShapeDtypeStruct((16, BLK), jnp.int32),
        ),
        in_specs=[smem, hbm, hbm, hbm, hbm, hbm],
        out_specs=(hbm,) * 3,
        scratch_shapes=[
            pltpu.VMEM(out_grad.shape, BF16),
            pltpu.VMEM(gate_pre.shape, BF16),
            pltpu.VMEM(up_pre.shape, BF16),
            pltpu.VMEM(mask.shape, jnp.int32),
            pltpu.VMEM((CAP, BLK, BLK), BF16),
            pltpu.VMEM((fs, cols * tok, BLK), BF16),
            pltpu.VMEM((fs, cols * tok, BLK), BF16),
            pltpu.VMEM((cols, fs * tok, BLK), BF16),
            pltpu.VMEM((groups, ts, per_z, fs * tok, BLK), BF16),
            pltpu.VMEM((groups, ts, per_z, fs * tok, BLK), BF16),
            pltpu.VMEM(blocks, BF16),
            pltpu.VMEM(slots, BF16),
            pltpu.VMEM(slots, BF16),
            pltpu.VMEM(halves, BF16),
            pltpu.VMEM(halves, BF16),
            pltpu.VMEM((cols, row_blocks, BLK, BLK), BF16),
            pltpu.VMEM((ts, 16, BLK), jnp.int32),
            pltpu.SMEM((ts, 16, BLK), jnp.int32),
            dma((4,)),
            dma((3,)),
            dma((cols,)),
            dma,
            dma((ts,)),
            dma((ts,)),
            dma((fs,)),
            dma((fs,)),
            dma((groups, ts)),
            dma((groups, ts)),
            dma((fs,)),
            dma((fs,)),
            dma((groups, fs)),
            dma((groups, fs)),
        ],
        compiler_params=pltpu.CompilerParams(
            collective_id=0, has_side_effects=True, vmem_limit_bytes=60 * 1024 * 1024
        ),
        name="exchange",
    )(live_rows, out_grad, gate_pre, up_pre, mask, down_weight.reshape(row_blocks, BLK, cols * BLK))
    return pl.pallas_call(
        functools.partial(finish_kernel, fs),
        out_shape=(
            jax.ShapeDtypeStruct(gate_pre.shape, BF16),
            jax.ShapeDtypeStruct(up_pre.shape, BF16),
            jax.ShapeDtypeStruct(down_weight.shape, BF16),
        ),
        in_specs=[smem, hbm, hbm, hbm, hbm],
        out_specs=(hbm, hbm, hbm),
        scratch_shapes=[
            pltpu.VMEM(halves, BF16),
            pltpu.VMEM((CAP, BLK, BLK), BF16),
            pltpu.VMEM(gate_pre.shape, BF16),
            pltpu.VMEM(up_pre.shape, BF16),
            pltpu.VMEM(blocks, F32),
            pltpu.VMEM((BLK, down_weight.shape[1]), BF16),
            pltpu.VMEM((CAP, BLK, down_weight.shape[1]), BF16),
            pltpu.VMEM(gate_pre.shape, BF16),
            pltpu.VMEM(up_pre.shape, BF16),
            dma((4,)),
            dma((row_blocks,)),
            dma((CAP,)),
            dma((2,)),
        ],
        compiler_params=pltpu.CompilerParams(vmem_limit_bytes=60 * 1024 * 1024),
        name="finish",
    )(lists, prod, tiles, gate_pre, up_pre)


def solution(mesh):
    return jax.shard_map(
        per_device,
        mesh=mesh,
        in_specs=(
            P(("fsdp", "tensor"), None),
            P(("fsdp", "tensor")),
            P("fsdp", "tensor"),
            P("fsdp", "tensor"),
            P("tensor", "fsdp"),
            P("tensor", None),
        ),
        out_specs=(P("fsdp", "tensor"), P("fsdp", "tensor"), P("tensor", "fsdp")),
        check_vma=False,
    )
```

time: 30.7 us -> 28.3 us (0.922)
  local copies, waits for them, and re-layouts: 3.46 us -> 0 us
  Pallas kernels: 25.7 us -> 26.8 us
    unnamed x8 -> x0, local copies, waits for them, and re-layouts: 3.46 us -> none
    pallas_call x1, Pallas kernels: 20.8 us -> 22.6 us  [per_device(): pl.pallas_call(functools.partial(exchange_kernel, fs, ts, cols, scale), o...]
    pallas_call x1, Pallas kernels: 4.95 us -> 4.23 us  [per_device(): pl.pallas_call(functools.partial(finish_kernel, fs), out_shape=(jax.Shape...]
where the time goes in v2:
time: 28.3 us; the launch traced here: 28.1 us
  Pallas kernels  26.8 us (95%)
  between operations  1.28 us (5%)
    pallas_call x1, Pallas kernels, per_device(): pl.pallas_call(functools.partial(exchange_kernel, fs, ts, cols, scale), o...  22.6 us
    pallas_call x1, Pallas kernels, per_device(): pl.pallas_call(functools.partial(finish_kernel, fs), out_shape=(jax.Shape...  4.23 us

profile of v2, /device:TPU:0, one launch (start us, length us, event | category | flops | bytes accessed | tf_op | source)
XLA Modules:
  0.0 28.1 jit_solution(14805148431961630424)
XLA Ops:
  1.3 22.6 %exchange.1 = (bf16[2,8,2,32,128]{4,3,2,1,0:T(8,128)(2,1)}, bf16[4,128,128]{2,1,0:T(8,128)(2,1)}, s32[16,128]{1,0:T(8,128)}) custom-call(s32[1]{0:T(128)S(6)} %copy.9.live_ref, bf16[8,8192]{1,0:T(8,128)(2,1)} %grad_hbm.1, bf16[32,3072]{1,0:T(8,128)(2,1)} %gate_hbm.3, bf16[32,3072]{1,0:T(8,128)(2,1)} %up_hbm.3, s32[24,64]{1,0:T(8,128)} %mask_hbm.1, ...), custom_call_target="tpu_custom_call" | custom-call | tf_op jit(solution)/shard_map/exchange/pallas_call | solution.py:325
  23.8 4.2 %finish.1 = (bf16[32,3072]{1,0:T(8,128)(2,1)}, bf16[32,3072]{1,0:T(8,128)(2,1)}, bf16[3072,1024]{1,0:T(8,128)(2,1)}) custom-call(s32[16,128]{1,0:T(8,128)} %get-tuple-element.6.idx_ref, bf16[2,8,2,32,128]{4,3,2,1,0:T(8,128)(2,1)} %get-tuple-element.7.prod_hbm, bf16[4,128,128]{2,1,0:T(8,128)(2,1)} %get-tuple-element.8.dw_hbm, bf16[32,3072]{1,0:T(8,128)(2,1)} %gate_hbm.3, ...), custom_call_target="tpu_custom_call" | custom-call | tf_op jit(solution)/shard_map/finish/pallas_call | solution.py:373
